TPU v7x, 256 devices: a whole 4x4x8 slice. The times are simulated.
256 devices in a mesh: row: 64 (over z, x, core), col: 4 (over y).
Axes of the slice: x: 4, y: 4, z: 8, core: 2. Of those that a mesh axis runs over, the one named last changes fastest.
Arguments:
- slab: bfloat16 [180224, 8192], P('row', 'col'), may hold values from -70 to 70, as said below
- test_matrix: bfloat16 [8192, 128], P('col'), may hold values from -0.0625 to 0.0625
Outputs:
- basis: bfloat16 [180224, 128], P('row')
- projected: float32 [8192, 128], P(('col', 'row'))
Inputs may be any that keep to these rules, and one draw needn't show every extreme that they name: Every entry is finite, and the sketch (slab times test_matrix) has full column rank.
All inputs are finite; a program needn't handle non-finite values.
Results may differ from a plain program's by a relative error of at most 0.004.
Values may be sent and summed in bfloat16 or wider, within the bound.
No kernel may reach another device: no remote copies, remote signals or barrier semaphores. Data moves between devices by JAX's collectives and lax.ppermute only.
A program may use at most 128 MiB of HBM per device.

v0:
```python
import jax
import jax.numpy as jnp
from jax import lax
from jax.sharding import PartitionSpec as P


def square_sum(left, right):
    return jnp.dot(
        left.T, right, precision=lax.Precision.HIGHEST, preferred_element_type=jnp.float32
    )


def body(slab, test_matrix):
    rows, columns = slab.shape
    width = test_matrix.shape[1]
    col_count = lax.axis_size("col")
    row_count = lax.axis_size("row")
    total_rows = rows * row_count
    quarter = rows // col_count
    partial_value = jnp.dot(slab, test_matrix, preferred_element_type=jnp.float32)
    whole_sketch = lax.psum(partial_value, "col")
    own_sketch = lax.dynamic_slice_in_dim(whole_sketch, lax.axis_index("col") * quarter, quarter, 0)
    local_gram = square_sum(own_sketch, own_sketch)
    gram = lax.psum(local_gram, ("row", "col")) / total_rows
    lower = jnp.linalg.cholesky(gram)
    identity = jnp.eye(width, dtype=jnp.float32)
    inverse = jax.scipy.linalg.solve_triangular(lower, identity, lower=True).T
    basis = jnp.dot(
        whole_sketch, inverse, precision=lax.Precision.HIGHEST, preferred_element_type=jnp.float32
    ).astype(jnp.bfloat16)
    factor = 1.0 / jnp.sqrt(jnp.float32(total_rows))
    projected = lax.psum_scatter(
        lax.dot_general(slab, basis, (((0,), (0,)), ((), ())), preferred_element_type=jnp.float32)
        * factor,
        "row",
        scatter_dimension=0,
        tiled=True,
    )
    return (basis, projected)


def solution(mesh):
    placed = (P("row", "col"), P("col", None))
    return jax.shard_map(
        body,
        mesh=mesh,
        in_specs=placed,
        out_specs=(P("row", None), P(("col", "row"), None)),
        check_vma=False,
    )
```

profile of v0, /device:TPU:1, one launch (start us, length us, event | category | flops | bytes accessed | tf_op | source)
XLA Modules:
  0.0 490.0 jit_solution(11114873559448150635)
XLA Ops:
  7.2 0.0 copy-start
  7.2 0.0 all-reduce.3.cloned.1.call-start
  7.2 1.0 copy-done
  8.2 7.1 %fusion.8 = f32[2816,128]{1,0:T(8,128)} fusion(bf16[2816,2048]{1,0:T(8,128)(2,1)} %param.2, bf16[2048,128]{1,0:T(8,128)(2,1)S(1)} %copy-done), kind=kOutput, calls=%fused_computation.17 | convolution fusion | flops 1476395008 | bytes 13500416 | tf_op jit(solution)/shard_map/dot_general | solution.py:20
  15.3 0.0 all-reduce.3.cloned.1.call-update
  15.3 0.0 all-reduce.5.cloned.1.call-start
  15.4 57.6 %all-reduce.3.cloned.1.call-done = f32[2816,128]{1,0:T(8,128)} async-done(((f32[2816,128]{1,0:T(8,128)}), f32[2816,128]{1,0:T(8,128)}) %all-reduce.3.cloned.1.call-update) | async-done | bytes 1441808 | tf_op jit(solution)/shard_map/psum | solution.py:21
  73.0 2.5 fusion.1
  75.5 0.0 all-reduce.5.cloned.1.call-update
  75.5 0.2 reduce-scatter.4.cloned.1.call-start
  75.7 242.3 %all-reduce.5.cloned.1.call-done = f32[128,128]{0,1:T(8,128)} async-done(((f32[128,128]{0,1:T(8,128)}), f32[128,128]{0,1:T(8,128)}) %all-reduce.5.cloned.1.call-update) | async-done | bytes 65552 | tf_op jit(solution)/shard_map/psum | solution.py:24
  318.0 0.8 broadcast_multiply_fusion
  318.9 0.1 copy.8
  319.0 0.9 fusion.6
  319.8 11.7 %cholesky.17 = f32[128,128]{1,0:T(8,128)S(1)} custom-call(f32[128,128]{1,0:T(8,128)S(1)} %fusion.6), custom_call_target="Cholesky" | custom-call | tf_op jit(solution)/shard_map/jit(cholesky)/cholesky | solution.py:25
  331.6 0.6 compare_reduce_fusion
  332.2 0.7 fusion.3
  332.9 9.8 %custom-call.7 = f32[1,128,128]{1,2,0:T(8,128)S(1)} custom-call(f32[1,128,128]{2,1,0:T(8,128)S(1)} %fusion.3), custom_call_target="InvertDiagBlocksLowerTriangular" | custom-call | tf_op jit(solution)/shard_map/jit(_solve_triangular)/triangular_solve | solution.py:27
  342.7 0.2 fusion.4
  342.9 2.7 convolution_convert_fusion
  345.6 6.2 %fusion = f32[2048,128]{0,1:T(8,128)S(1)} fusion(bf16[2816,128]{1,0:T(8,128)(2,1)S(1)} %convolution_convert_fusion, bf16[2816,2048]{1,0:T(8,128)(2,1)} %param.2), kind=kOutput, calls=%fused_computation.2 | convolution fusion | flops 1476657152 | bytes 13303808 | tf_op jit(solution)/shard_map/dot_general | solution.py:33
  351.9 1.3 copy.11
  353.2 0.0 reduce-scatter.4.cloned.1.call-update
  353.2 130.2 %reduce-scatter.4.cloned.1.call-done = f32[32,128]{1,0:T(8,128)} async-done(((f32[2048,128]{1,0:T(8,128)}), f32[32,128]{1,0:T(8,128)}) %reduce-scatter.4.cloned.1.call-update) | async-done | bytes 16400
  (3 shorter events, 0.0 us)
Async XLA Ops:
  7.2 1.0 copy-start
  7.2 65.8 %all-reduce.3.cloned.1.call-start = ((), (), s32[]{:S(2)}) async-start(), calls=%async_computation.1 | async-start | bytes 2883584 | tf_op jit(solution)/shard_map/psum | solution.py:21
  15.3 302.7 %all-reduce.5.cloned.1.call-start = ((), (), s32[]{:S(2)}) async-start(), calls=%async_computation.2 | async-start | bytes 131072 | tf_op jit(solution)/shard_map/psum | solution.py:24
  75.5 407.9 %reduce-scatter.4.cloned.1.call-start = ((), (), s32[]{:S(2)}) async-start(), calls=%async_computation.3 | async-start | bytes 1064960
  345.6 6.2 %copy-start.1 = (bf16[2816,128]{1,0:T(8,128)(2,1)}, bf16[2816,128]{1,0:T(8,128)(2,1)S(1)}, u32[]{:S(2)}) copy-start(bf16[2816,128]{1,0:T(8,128)(2,1)S(1)} %convolution_convert_fusion) | copy-start | bytes 2162692
Sparse Core Ops, SparseCore 0:
  15.5 57.4 all-reduce.2
  79.0 238.9 all-reduce.4
  353.3 130.0 reduce-scatter.3
where the time goes:
time: 495 us; the launch traced here: 490 us
  waiting for transfers between devices  430 us (87%)
  other arithmetic  24.6 us (5%)
  matrix products  18.8 us (4%)
  between operations  13.8 us (3%)
    psum x1, waiting for transfers between devices, body(): gram = lax.psum(local_gram, ('row', 'col')) / total_rows  242 us
    unnamed x4, waiting for transfers between devices  130 us
    psum x1, waiting for transfers between devices, body(): whole_sketch = lax.psum(partial_value, 'col')  57.6 us
    another operation x3, other arithmetic, body(): lower = jnp.linalg.cholesky(gram)  12.4 us
    another operation x2, other arithmetic, body(): inverse = jax.scipy.linalg.solve_triangular(lower, identity, lower=True).T  10.5 us
  transfers between devices with their start and end apart: 3, of which 3 were waited for; matrix products, arithmetic and copies ran while one was open for 0% of the time, Pallas kernels for 0%

commit v1 on v0

v1 whole, which is shorter than its diff:
```python
import jax
import jax.numpy as jnp
from jax import lax
from jax.sharding import PartitionSpec as P

Z, X, C, Y = 8, 4, 2, 4


def row_of(z, x, c):
    return ((z % Z) * X + x % X) * C + c % C


def row_shift(value, dz, dx, dc):
    pairs = [
        (row_of(z, x, c), row_of(z + dz, x + dx, c + dc))
        for z in range(Z)
        for x in range(X)
        for c in range(C)
    ]
    return lax.ppermute(value, "row", pairs)


def col_shift(value, dy):
    return lax.ppermute(value, "col", [(y, (y + dy) % Y) for y in range(Y)])


def body(slab, test_matrix):
    rows, columns = slab.shape
    width = test_matrix.shape[1]
    total_rows = rows * lax.axis_size("row")
    quarter = rows // Y
    me_y = lax.axis_index("col")
    row = lax.axis_index("row")
    me_c, me_x = row % C, (row // C) % X

    def part(shift):
        start = ((me_y + shift) % Y) * quarter
        block = lax.dynamic_slice_in_dim(slab, start, quarter, 0)
        return jnp.dot(block, test_matrix, preferred_element_type=jnp.float32)

    received = [col_shift(part(dy), dy) for dy in (2, 1, 3)]
    own = part(0)
    for piece in received:
        own = own + piece
    own = own.astype(jnp.bfloat16)

    pieces = [own] + [col_shift(own, dy) for dy in (1, 2, 3)]
    sketch = jnp.zeros((rows, width), jnp.bfloat16)
    for dy, piece in enumerate(pieces):
        sketch = lax.dynamic_update_slice_in_dim(sketch, piece, ((me_y - dy) % Y) * quarter, 0)

    dims = (((0,), (0,)), ((), ()))
    product = lax.dot_general(slab, sketch, dims, preferred_element_type=jnp.float32)
    gram = lax.dot_general(sketch, sketch, dims, preferred_element_type=jnp.float32)

    half = width // C
    product = product.reshape(Z, X, C, 32, width)
    gram = gram.reshape(C, half, width)

    def pick(array, index, axis):
        return lax.dynamic_index_in_dim(array, index, axis, keepdims=False)

    def joined(a, b):
        return jnp.concatenate([a.reshape(-1, width), b], 0)

    state = joined(pick(product, me_c, 2), pick(gram, me_c, 0))
    state = state + row_shift(joined(pick(product, 1 - me_c, 2), pick(gram, 1 - me_c, 0)), 0, 0, 1)

    product, gram = state[:-half].reshape(Z, X, 32, width), state[-half:]
    state = joined(pick(product, me_x, 1), gram)
    for dx in (2, 1, 3):
        state = state + row_shift(joined(pick(product, (me_x + dx) % X, 1), gram), 0, dx, 0)

    product, gram = state[:-half].reshape(Z, 32, width), state[-half:]
    packed = jnp.concatenate([product, jnp.broadcast_to(gram[None], (Z, half, width))], 1)
    groups = [[row_of(z, x, c) for z in range(Z)] for x in range(X) for c in range(C)]
    packed = lax.all_to_all(packed, "row", 0, 0, axis_index_groups=groups)
    state = jnp.sum(packed, 0)
    product, gram = state[:32], state[32:]
    other = row_shift(gram, 0, 0, 1)
    gram = jnp.where(me_c == 0, jnp.concatenate([gram, other], 0), jnp.concatenate([other, gram], 0))

    lower = jnp.linalg.cholesky(gram / total_rows)
    identity = jnp.eye(width, dtype=jnp.float32)
    inverse = jax.scipy.linalg.solve_triangular(lower, identity, lower=True).T
    high = inverse.astype(jnp.bfloat16)
    low = (inverse - high.astype(jnp.float32)).astype(jnp.bfloat16)
    basis = jnp.dot(sketch, high, preferred_element_type=jnp.float32)
    basis = basis + jnp.dot(sketch, low, preferred_element_type=jnp.float32)
    factor = 1.0 / jnp.sqrt(jnp.float32(total_rows))
    projected = jnp.dot(product, inverse * factor, precision=lax.Precision.HIGHEST)
    return (basis.astype(jnp.bfloat16), projected)


def solution(mesh):
    placed = (P("row", "col"), P("col", None))
    return jax.shard_map(
        body,
        mesh=mesh,
        in_specs=placed,
        out_specs=(P("row", None), P(("col", "row"), None)),
        check_vma=False,
    )
```

time: 495 us -> 113 us (0.23)
  waiting for transfers between devices: 430 us -> 19.8 us
  starting transfers between devices: 0.3 us -> 25 us
  blocking collectives: 0 us -> 21.7 us
  between operations: 13.8 us -> 0.88 us
    psum x2 -> x0, waiting for transfers between devices: 300 us -> none  [the longest x1 242 us: body(): gram = lax.psum(local_gram, ('row', 'col')) / total_rows]
    unnamed x4 -> x0, waiting for transfers between devices: 130 us -> none
    ppermute x0 -> x11, starting transfers between devices: none -> 25 us  [the longest x6 13.3 us: col_shift(): return lax.ppermute(value, 'col', [(y, (y + dy) % Y) for y in range(Y)])]
    all_to_all x0 -> x1, blocking collectives: none -> 21.7 us  [body(): packed = lax.all_to_all(packed, 'row', 0, 0, axis_index_groups=groups)]
    ppermute x0 -> x11, waiting for transfers between devices: none -> 19.8 us  [the longest x6 12.2 us: col_shift(): return lax.ppermute(value, 'col', [(y, (y + dy) % Y) for y in range(Y)])]
    dot_general x4 -> x9, matrix products: 18.5 us -> 19.6 us  [the longest x4 11 us: part(): return jnp.dot(block, test_matrix, preferred_element_type=jnp.float32)]
  transfers between devices with their start and end apart: 3 -> 11, of which waited for: 3 -> 8; matrix products, arithmetic and copies ran while one was open for 0% -> 5% of each run, Pallas kernels for 0% -> 0%
where the time goes in v1:
time: 113 us; the launch traced here: 112 us
  starting transfers between devices  25 us (22%)
  other arithmetic  23.2 us (21%)
  blocking collectives  21.7 us (19%)
  matrix products  19.9 us (18%)
  waiting for transfers between devices  19.8 us (18%)
  local copies, waits for them, and re-layouts  1.93 us (2%)
    all_to_all x1, blocking collectives, body(): packed = lax.all_to_all(packed, 'row', 0, 0, axis_index_groups=groups)  21.7 us
    ppermute x6, starting transfers between devices, col_shift(): return lax.ppermute(value, 'col', [(y, (y + dy) % Y) for y in range(Y)])  13.3 us
    another operation x3, other arithmetic, body(): lower = jnp.linalg.cholesky(gram / total_rows)  12.4 us
    ppermute x6, waiting for transfers between devices, col_shift(): return lax.ppermute(value, 'col', [(y, (y + dy) % Y) for y in range(Y)])  12.2 us
    ppermute x5, starting transfers between devices, row_shift(): return lax.ppermute(value, 'row', pairs)  11.7 us
    dot_general x4, matrix products, part(): return jnp.dot(block, test_matrix, preferred_element_type=jnp.float32)  11 us
    another operation x2, other arithmetic, body(): inverse = jax.scipy.linalg.solve_triangular(lower, identity, lower=True).T  10.5 us
    ppermute x5, waiting for transfers between devices, row_shift(): return lax.ppermute(value, 'row', pairs)  7.57 us
  transfers between devices with their start and end apart: 11, of which 8 were waited for; matrix products, arithmetic and copies ran while one was open for 5% of the time, Pallas kernels for 0%

profile of v1, /device:TPU:1, one launch (start us, length us, event | category | flops | bytes accessed | tf_op | source)
XLA Modules:
  0.0 112.3 jit_solution(12442881373779299667)
XLA Ops:
  1.7 2.7 %fusion.3 = f32[704,128]{1,0:T(8,128)S(1)} fusion(bf16[2048,128]{1,0:T(8,128)(2,1)S(1)} %copy-done, bf16[2816,2048]{1,0:T(8,128)(2,1)} %param.2, s32[]{:T(128)S(6)} %select_n.119), kind=kOutput, calls=%fused_computation.4 | convolution fusion | flops 369098752 | bytes 3768324 | tf_op jit(solution)/shard_map/dot_general | solution.py:39
  4.4 2.2 %collective-permute-start.1 = (f32[704,128]{1,0:T(8,128)S(1)}, f32[704,128]{1,0:T(8,128)S(1)}, u32[]{:S(2)}, u32[]{:S(2)}) collective-permute-start(f32[704,128]{1,0:T(8,128)S(1)} %fusion.3), channel_id=1, source_target_pairs={{0,1},{1,2},{2,3},{3,0},{4,5},{5,6},{6,7},{7,4},{8,9},{9,10},{10,1... | collective-permute-start | bytes 1081352 | tf_op jit(solution)/shard_map/ppermute | solution.py:24
  6.6 2.7 %fusion.1 = f32[704,128]{1,0:T(8,128)S(1)} fusion(bf16[2048,128]{1,0:T(8,128)(2,1)S(1)} %copy-done, bf16[2816,2048]{1,0:T(8,128)(2,1)} %param.2, s32[]{:T(128)S(6)} %select_n.121), kind=kOutput, calls=%fused_computation.2 | convolution fusion | flops 369098752 | bytes 3768324 | tf_op jit(solution)/shard_map/dot_general | solution.py:39
  9.3 1.6 %collective-permute-start.2 = (f32[704,128]{1,0:T(8,128)S(1)}, f32[704,128]{1,0:T(8,128)S(1)}, u32[]{:S(2)}, u32[]{:S(2)}) collective-permute-start(f32[704,128]{1,0:T(8,128)S(1)} %fusion.1), channel_id=1, source_target_pairs={{0,3},{1,0},{2,1},{3,2},{4,7},{5,4},{6,5},{7,6},{8,11},{9,8},{10,9... | collective-permute-start | bytes 1081352 | tf_op jit(solution)/shard_map/ppermute | solution.py:24
  10.9 2.7 %fusion.5 = f32[704,128]{1,0:T(8,128)S(1)} fusion(bf16[2048,128]{1,0:T(8,128)(2,1)S(1)} %copy-done, bf16[2816,2048]{1,0:T(8,128)(2,1)} %param.2, s32[]{:T(128)S(6)} %select_n.117), kind=kOutput, calls=%fused_computation.6 | convolution fusion | flops 369098752 | bytes 3768324 | tf_op jit(solution)/shard_map/dot_general | solution.py:39
  13.6 1.7 %collective-permute-start = (f32[704,128]{1,0:T(8,128)S(1)}, f32[704,128]{1,0:T(8,128)S(1)}, u32[]{:S(2)}, u32[]{:S(2)}) collective-permute-start(f32[704,128]{1,0:T(8,128)S(1)} %fusion.5), channel_id=1, source_target_pairs={{0,2},{1,3},{2,0},{3,1},{4,6},{5,7},{6,4},{7,5},{8,10},{9,11},{10,... | collective-permute-start | bytes 1081352 | tf_op jit(solution)/shard_map/ppermute | solution.py:24
  15.3 2.9 %collective-permute-done.2 = f32[704,128]{1,0:T(8,128)S(1)} collective-permute-done((f32[704,128]{1,0:T(8,128)S(1)}, f32[704,128]{1,0:T(8,128)S(1)}, u32[]{:S(2)}, u32[]{:S(2)}) %collective-permute-start.2) | collective-permute-done | bytes 360480 | tf_op jit(solution)/shard_map/ppermute | solution.py:24
  18.2 4.7 %collective-permute-done = f32[704,128]{1,0:T(8,128)S(1)} collective-permute-done((f32[704,128]{1,0:T(8,128)S(1)}, f32[704,128]{1,0:T(8,128)S(1)}, u32[]{:S(2)}, u32[]{:S(2)}) %collective-permute-start) | collective-permute-done | bytes 360480 | tf_op jit(solution)/shard_map/ppermute | solution.py:24
  22.9 2.8 %constant_dynamic-update-slice_fusion.3 = (bf16[2816,128]{1,0:T(8,128)(2,1)S(1)}, bf16[704,128]{1,0:T(8,128)(2,1)S(1)}) fusion(bf16[2816,128]{1,0:T(8,128)(2,1)S(1)} %broadcast_in_dim.5, s32[]{:T(128)S(6)} %select_n.115, f32[704,128]{1,0:T(8,128)S(1)} %collective-permute-done.2, f32[704,128]{1,0:T(8,128)S(1)} %collective-permute-done.1, ...), kind=kOutput, calls=%fused_computation.55 | convolution fusion | flops 369459200 | bytes 4850688 | tf_op jit(solution)/shard_map/dot_general | solution.py:39
  25.7 5.4 %collective-permute-start.3 = (bf16[704,128]{1,0:T(8,128)(2,1)S(1)}, bf16[704,128]{1,0:T(8,128)(2,1)S(1)}, u32[]{:S(2)}, u32[]{:S(2)}) collective-permute-start(bf16[704,128]{1,0:T(8,128)(2,1)S(1)} %get-tuple-element.14), channel_id=1, source_target_pairs={{0,1},{1,2},{2,3},{3,0},{4,5},{5,6},{6,7},{7,4},{8,9},{9,10},{10,1... | collective-permute-start | bytes 540680 | tf_op jit(solution)/shard_map/ppermute | solution.py:24
  31.1 1.4 %collective-permute-start.4 = (bf16[704,128]{1,0:T(8,128)(2,1)S(1)}, bf16[704,128]{1,0:T(8,128)(2,1)S(1)}, u32[]{:S(2)}, u32[]{:S(2)}) collective-permute-start(bf16[704,128]{1,0:T(8,128)(2,1)S(1)} %get-tuple-element.14), channel_id=1, source_target_pairs={{0,2},{1,3},{2,0},{3,1},{4,6},{5,7},{6,4},{7,5},{8,10},{9,11},{10,... | collective-permute-start | bytes 540680 | tf_op jit(solution)/shard_map/ppermute | solution.py:24
  34.2 4.1 %collective-permute-done.4 = bf16[704,128]{1,0:T(8,128)(2,1)S(1)} collective-permute-done((bf16[704,128]{1,0:T(8,128)(2,1)S(1)}, bf16[704,128]{1,0:T(8,128)(2,1)S(1)}, u32[]{:S(2)}, u32[]{:S(2)}) %collective-permute-start.4) | collective-permute-done | bytes 180256 | tf_op jit(solution)/shard_map/ppermute | solution.py:24
  38.8 6.0 %convolution_bitcast_fusion = f32[2048,128]{0,1:T(8,128)S(1)} fusion(bf16[2816,128]{1,0:T(8,128)(2,1)S(1)} %constant_dynamic-update-slice_fusion, bf16[2816,2048]{1,0:T(8,128)(2,1)} %param.2), kind=kOutput, calls=%fused_computation.10 | convolution fusion | flops 1476395008 | bytes 13303808 | tf_op jit(solution)/shard_map/dot_general | solution.py:53
  45.3 3.6 %collective-permute-start.6 = (f32[1088,128]{1,0:T(8,128)S(1)}, f32[1088,128]{1,0:T(8,128)S(1)}, u32[]{:S(2)}, u32[]{:S(2)}) collective-permute-start(f32[1088,128]{1,0:T(8,128)S(1)} %pad_maximum_fusion), channel_id=1, source_target_pairs={{0,4},{4,0},{8,12},{12,8},{16,20},{20,16},{24,28},{28,24},{32,36},... | collective-permute-start | bytes 1671176 | tf_op jit(solution)/shard_map/ppermute | solution.py:20
  48.9 1.6 %collective-permute-done.6 = f32[1088,128]{1,0:T(8,128)S(1)} collective-permute-done((f32[1088,128]{1,0:T(8,128)S(1)}, f32[1088,128]{1,0:T(8,128)S(1)}, u32[]{:S(2)}, u32[]{:S(2)}) %collective-permute-start.6) | collective-permute-done | bytes 557088 | tf_op jit(solution)/shard_map/ppermute | solution.py:20
  50.7 3.0 %collective-permute-start.7 = (f32[320,128]{1,0:T(8,128)S(1)}, f32[320,128]{1,0:T(8,128)S(1)}, u32[]{:S(2)}, u32[]{:S(2)}) collective-permute-start(f32[320,128]{1,0:T(8,128)S(1)} %get-tuple-element.10), channel_id=1, source_target_pairs={{0,16},{4,20},{8,24},{12,28},{16,0},{20,4},{24,8},{28,12},{32,48},... | collective-permute-start | bytes 491528 | tf_op jit(solution)/shard_map/ppermute | solution.py:20
  54.0 2.4 %collective-permute-start.9 = (f32[320,128]{1,0:T(8,128)S(1)}, f32[320,128]{1,0:T(8,128)S(1)}, u32[]{:S(2)}, u32[]{:S(2)}) collective-permute-start(f32[320,128]{1,0:T(8,128)S(1)} %get-tuple-element.12), channel_id=1, source_target_pairs={{0,24},{4,28},{8,0},{12,4},{16,8},{20,12},{24,16},{28,20},{32,56},... | collective-permute-start | bytes 491528 | tf_op jit(solution)/shard_map/ppermute | solution.py:20
  56.4 1.3 %collective-permute-done.7 = f32[320,128]{1,0:T(8,128)S(1)} collective-permute-done((f32[320,128]{1,0:T(8,128)S(1)}, f32[320,128]{1,0:T(8,128)S(1)}, u32[]{:S(2)}, u32[]{:S(2)}) %collective-permute-start.7) | collective-permute-done | bytes 163872 | tf_op jit(solution)/shard_map/ppermute | solution.py:20
  57.7 3.8 %collective-permute-done.8 = f32[320,128]{1,0:T(8,128)S(1)} collective-permute-done((f32[320,128]{1,0:T(8,128)S(1)}, f32[320,128]{1,0:T(8,128)S(1)}, u32[]{:S(2)}, u32[]{:S(2)}) %collective-permute-start.8) | collective-permute-done | bytes 163872 | tf_op jit(solution)/shard_map/ppermute | solution.py:20
  61.6 21.7 %all_to_all.5 = f32[8,96,128]{2,1,0:T(8,128)S(1)} all-to-all(f32[8,96,128]{2,1,0:T(8,128)S(1)} %pad_maximum_fusion.1), channel_id=1, replica_groups={{0,32,64,96,128,160,192,224},{4,36,68,100,132,164,196,228},{8,40,72,104..., dimensions={0} | all-to-all | bytes 786432 | tf_op jit(solution)/shard_map/all_to_all | solution.py:77
  83.4 2.4 %collective-permute-start.10 = (f32[64,128]{0,1:T(8,128)S(1)}, f32[64,128]{0,1:T(8,128)S(1)}, u32[]{:S(2)}, u32[]{:S(2)}) collective-permute-start(f32[64,128]{0,1:T(8,128)S(1)} %copy.17), channel_id=1, source_target_pairs={{0,4},{4,0},{8,12},{12,8},{16,20},{20,16},{24,28},{28,24},{32,36},... | collective-permute-start | bytes 98312 | tf_op jit(solution)/shard_map/ppermute | solution.py:20
  86.9 11.7 %cholesky.14 = f32[128,128]{1,0:T(8,128)S(1)} custom-call(f32[128,128]{1,0:T(8,128)S(1)} %fusion.28), custom_call_target="Cholesky" | custom-call | tf_op jit(solution)/shard_map/jit(cholesky)/cholesky | solution.py:83
  100.0 9.8 %custom-call.7 = f32[1,128,128]{1,2,0:T(8,128)S(1)} custom-call(f32[1,128,128]{2,1,0:T(8,128)S(1)} %fusion.24), custom_call_target="InvertDiagBlocksLowerTriangular" | custom-call | tf_op jit(solution)/shard_map/jit(_solve_triangular)/triangular_solve | solution.py:85
  111.1 1.2 %fusion = bf16[2816,128]{1,0:T(8,128)(2,1)} fusion(f32[2816,128]{1,0:T(8,128)S(1)} %fusion.31, bf16[2816,128]{1,0:T(8,128)(2,1)S(1)} %constant_dynamic-update-slice_fusion, f32[128,128]{1,0:T(8,128)S(1)} %fusion.26), kind=kOutput, calls=%fused_computation.1 | convolution fusion | flops 93011968 | bytes 2949120 | tf_op jit(solution)/shard_map/dot_general | solution.py:88
  (40 shorter events, 8.3 us)
Async XLA Ops:
  0.6 1.0 copy-start
  4.4 10.9 %collective-permute-start.1 = (f32[704,128]{1,0:T(8,128)S(1)}, f32[704,128]{1,0:T(8,128)S(1)}, u32[]{:S(2)}, u32[]{:S(2)}) collective-permute-start(f32[704,128]{1,0:T(8,128)S(1)} %fusion.3), channel_id=1, source_target_pairs={{0,1},{1,2},{2,3},{3,0},{4,5},{5,6},{6,7},{7,4},{8,9},{9,10},{10,1... | collective-permute-start | bytes 1081352 | tf_op jit(solution)/shard_map/ppermute | solution.py:24
  9.3 8.8 %collective-permute-start.2 = (f32[704,128]{1,0:T(8,128)S(1)}, f32[704,128]{1,0:T(8,128)S(1)}, u32[]{:S(2)}, u32[]{:S(2)}) collective-permute-start(f32[704,128]{1,0:T(8,128)S(1)} %fusion.1), channel_id=1, source_target_pairs={{0,3},{1,0},{2,1},{3,2},{4,7},{5,4},{6,5},{7,6},{8,11},{9,8},{10,9... | collective-permute-start | bytes 1081352 | tf_op jit(solution)/shard_map/ppermute | solution.py:24
  13.6 9.2 %collective-permute-start = (f32[704,128]{1,0:T(8,128)S(1)}, f32[704,128]{1,0:T(8,128)S(1)}, u32[]{:S(2)}, u32[]{:S(2)}) collective-permute-start(f32[704,128]{1,0:T(8,128)S(1)} %fusion.5), channel_id=1, source_target_pairs={{0,2},{1,3},{2,0},{3,1},{4,6},{5,7},{6,4},{7,5},{8,10},{9,11},{10,... | collective-permute-start | bytes 1081352 | tf_op jit(solution)/shard_map/ppermute | solution.py:24
  25.7 8.5 %collective-permute-start.3 = (bf16[704,128]{1,0:T(8,128)(2,1)S(1)}, bf16[704,128]{1,0:T(8,128)(2,1)S(1)}, u32[]{:S(2)}, u32[]{:S(2)}) collective-permute-start(bf16[704,128]{1,0:T(8,128)(2,1)S(1)} %get-tuple-element.14), channel_id=1, source_target_pairs={{0,1},{1,2},{2,3},{3,0},{4,5},{5,6},{6,7},{7,4},{8,9},{9,10},{10,1... | collective-permute-start | bytes 540680 | tf_op jit(solution)/shard_map/ppermute | solution.py:24
  31.1 7.2 %collective-permute-start.4 = (bf16[704,128]{1,0:T(8,128)(2,1)S(1)}, bf16[704,128]{1,0:T(8,128)(2,1)S(1)}, u32[]{:S(2)}, u32[]{:S(2)}) collective-permute-start(bf16[704,128]{1,0:T(8,128)(2,1)S(1)} %get-tuple-element.14), channel_id=1, source_target_pairs={{0,2},{1,3},{2,0},{3,1},{4,6},{5,7},{6,4},{7,5},{8,10},{9,11},{10,... | collective-permute-start | bytes 540680 | tf_op jit(solution)/shard_map/ppermute | solution.py:24
  32.5 5.9 %collective-permute-start.5 = (bf16[704,128]{1,0:T(8,128)(2,1)S(1)}, bf16[704,128]{1,0:T(8,128)(2,1)S(1)}, u32[]{:S(2)}, u32[]{:S(2)}) collective-permute-start(bf16[704,128]{1,0:T(8,128)(2,1)S(1)} %get-tuple-element.14), channel_id=1, source_target_pairs={{0,3},{1,0},{2,1},{3,2},{4,7},{5,4},{6,5},{7,6},{8,11},{9,8},{10,9... | collective-permute-start | bytes 540680 | tf_op jit(solution)/shard_map/ppermute | solution.py:24
  45.3 5.2 %collective-permute-start.6 = (f32[1088,128]{1,0:T(8,128)S(1)}, f32[1088,128]{1,0:T(8,128)S(1)}, u32[]{:S(2)}, u32[]{:S(2)}) collective-permute-start(f32[1088,128]{1,0:T(8,128)S(1)} %pad_maximum_fusion), channel_id=1, source_target_pairs={{0,4},{4,0},{8,12},{12,8},{16,20},{20,16},{24,28},{28,24},{32,36},... | collective-permute-start | bytes 1671176 | tf_op jit(solution)/shard_map/ppermute | solution.py:20
  50.7 7.0 %collective-permute-start.7 = (f32[320,128]{1,0:T(8,128)S(1)}, f32[320,128]{1,0:T(8,128)S(1)}, u32[]{:S(2)}, u32[]{:S(2)}) collective-permute-start(f32[320,128]{1,0:T(8,128)S(1)} %get-tuple-element.10), channel_id=1, source_target_pairs={{0,16},{4,20},{8,24},{12,28},{16,0},{20,4},{24,8},{28,12},{32,48},... | collective-permute-start | bytes 491528 | tf_op jit(solution)/shard_map/ppermute | solution.py:20
  53.7 7.8 %collective-permute-start.8 = (f32[320,128]{1,0:T(8,128)S(1)}, f32[320,128]{1,0:T(8,128)S(1)}, u32[]{:S(2)}, u32[]{:S(2)}) collective-permute-start(f32[320,128]{1,0:T(8,128)S(1)} %get-tuple-element.11), channel_id=1, source_target_pairs={{0,8},{4,12},{8,16},{12,20},{16,24},{20,28},{24,0},{28,4},{32,40},... | collective-permute-start | bytes 491528 | tf_op jit(solution)/shard_map/ppermute | solution.py:20
  54.0 7.5 %collective-permute-start.9 = (f32[320,128]{1,0:T(8,128)S(1)}, f32[320,128]{1,0:T(8,128)S(1)}, u32[]{:S(2)}, u32[]{:S(2)}) collective-permute-start(f32[320,128]{1,0:T(8,128)S(1)} %get-tuple-element.12), channel_id=1, source_target_pairs={{0,24},{4,28},{8,0},{12,4},{16,8},{20,12},{24,16},{28,20},{32,56},... | collective-permute-start | bytes 491528 | tf_op jit(solution)/shard_map/ppermute | solution.py:20
  83.4 3.3 %collective-permute-start.10 = (f32[64,128]{0,1:T(8,128)S(1)}, f32[64,128]{0,1:T(8,128)S(1)}, u32[]{:S(2)}, u32[]{:S(2)}) collective-permute-start(f32[64,128]{0,1:T(8,128)S(1)} %copy.17), channel_id=1, source_target_pairs={{0,4},{4,0},{8,12},{12,8},{16,20},{20,16},{24,28},{28,24},{32,36},... | collective-permute-start | bytes 98312 | tf_op jit(solution)/shard_map/ppermute | solution.py:20

commit v2 on v0

v2 whole, which is shorter than its diff:
```python
import jax
import jax.numpy as jnp
from jax import lax
from jax.experimental import pallas as pl
from jax.experimental.pallas import tpu as pltpu
from jax.sharding import PartitionSpec as P

Z, X, C, Y = 8, 4, 2, 4
F32, BF16, F16 = jnp.float32, jnp.bfloat16, jnp.float16
VMEM = pl.BlockSpec(memory_space=pltpu.VMEM)
SMEM = pl.BlockSpec(memory_space=pltpu.SMEM)
ANY = pl.BlockSpec(memory_space=pl.ANY)
MIB = 2**20
TAIL = 16


def row_of(z, x, c):
    return ((z % Z) * X + x % X) * C + c % C


def row_shift(value, dz, dx, dc):
    pairs = [
        (row_of(z, x, c), row_of(z + dz, x + dx, c + dc))
        for z in range(Z)
        for x in range(X)
        for c in range(C)
    ]
    return lax.ppermute(value, "row", pairs)


def col_shift(value, dy):
    return lax.ppermute(value, "col", [(y, (y + dy) % Y) for y in range(Y)])


def scaled(value):
    top = jnp.max(jnp.abs(value), axis=0, keepdims=True)
    exponent = jnp.floor(jnp.log2(jnp.maximum(top, 1e-30)))
    return value * jnp.exp2(-exponent), jnp.broadcast_to(exponent, (TAIL, value.shape[1]))


def unscaled(ref):
    rows = ref.shape[0] - TAIL
    return ref[0:rows, :] * jnp.exp2(ref[rows : rows + 1, :])


def sketch_kernel(me, slab, test, remote, own, held, sems):
    quarter = own.shape[0]
    parts = 2
    tile = quarter // parts
    starts = []
    for shift in (2, 1, 3, 0):
        base = lax.rem(me[0] + shift, Y) * quarter
        starts += [pl.multiple_of(base + t * tile, 16) for t in range(parts)]
    copies = [
        pltpu.make_async_copy(slab.at[pl.ds(s, tile)], held.at[pl.ds(s, tile)], sems.at[i])
        for i, s in enumerate(starts)
    ]
    copies[0].start()
    copies[1].start()
    for i, s in enumerate(starts):
        copies[i].wait()
        if i + 2 < len(copies):
            copies[i + 2].start()
        block, t = i // parts, i % parts
        value = jnp.dot(held[pl.ds(s, tile), :], test[...], preferred_element_type=F32)
        if block < 3:
            remote[block, t * tile : (t + 1) * tile, :] = value
        else:
            own[t * tile : (t + 1) * tile, :] = value
        if block < 3 and t == parts - 1:
            remote[block, 0:quarter, :], remote[block, quarter:, :] = scaled(
                remote[block, 0:quarter, :]
            )


def combine_kernel(own, a, b, c, out):
    rows = own.shape[0]
    total = own[...] + unscaled(a) + unscaled(b) + unscaled(c)
    out[0:rows, :], out[rows:, :] = scaled(total)


def product_kernel(me, slab, p0, p1, p2, p3, pieces, gram, sketch, flipped, product):
    quarter = p0.shape[0] - TAIL
    for shift, piece in enumerate((p0, p1, p2, p3)):
        start = pl.multiple_of(lax.rem(me[0] + Y - shift, Y) * quarter, 16)
        value = unscaled(piece)
        high = value.astype(BF16)
        sketch[pl.ds(start, quarter), 0:128] = high
        sketch[pl.ds(start, quarter), 128:256] = (value - high.astype(F32)).astype(BF16)
    flipped[...] = sketch[...].T
    full = jnp.dot(flipped[...], sketch[...], preferred_element_type=F32)
    full = full[0:128] + full[128:256]
    gram[...] = full[:, 0:128] + full[:, 128:256]
    product[...] = jnp.dot(flipped[0:128, :], slab[...], preferred_element_type=F32)
    for j in range(16):
        block = product[:, 128 * j : 128 * (j + 1)].T
        for i in range(4):
            r = 4 * j + i
            z, x, c = r // (X * C), (r // C) % X, r % C
            place = lax.rem(x + X - me[2], X) * Z + lax.rem(z + Z - me[1], Z)
            other = lax.rem(c + me[3], C)
            pieces[other, pl.ds(pl.multiple_of(place * 32, 32), 32), :] = block[32 * i : 32 * i + 32]


def inverse_rows(gram):
    lane = lax.broadcasted_iota(jnp.int32, (8, 128), 1)
    sub = lax.broadcasted_iota(jnp.int32, (8, 128), 0)
    work = [gram[8 * i : 8 * i + 8, :] for i in range(16)]
    out = []
    for b in range(16):
        c0 = 8 * b
        inside = (lane >= c0) & (lane < c0 + 8)
        panel = work[b]
        column = [jnp.broadcast_to(panel[:, c0 + c : c0 + c + 1], (8, 128)) for c in range(8)]
        panel = jnp.where(inside, (lane - c0 == sub).astype(F32), panel)
        root, upper, row = [], {}, []
        scale = jnp.zeros((8, 128), F32)
        for k in range(8):
            pivot = jnp.broadcast_to(column[k][k : k + 1, :], (8, 128))
            r = lax.rsqrt(pivot)
            r = r * (1.5 - 0.5 * pivot * r * r)
            root.append(r)
            row.append(jnp.broadcast_to(panel[k : k + 1, :], (8, 128)) * r)
            scale = jnp.where(sub == k, r, scale)
            if k < 7:
                m = jnp.where(sub > k, column[k] * r, 0.0)
                panel = panel - m * row[k]
                for c in range(k + 1, 8):
                    upper[k, c] = jnp.broadcast_to(column[c][k : k + 1, :], (8, 128)) * r
                    column[c] = column[c] - m * upper[k, c]
        out.append(jnp.where(lane <= sub + c0, panel * scale, 0.0))
        for i in range(b + 1, 16):
            left = [jnp.broadcast_to(work[i][:, c0 + c : c0 + c + 1], (8, 128)) for c in range(8)]
            rest = jnp.where(inside, 0.0, work[i])
            for k in range(8):
                m = left[k] * root[k]
                for c in range(k + 1, 8):
                    left[c] = left[c] - m * upper[k, c]
                rest = rest - m * row[k]
            work[i] = rest
    return out


def finish_kernel(total_rows, gram, sketch, product, basis, projected, factor, weights):
    rows = inverse_rows(gram[...] * (1.0 / total_rows))
    for i, value in enumerate(rows):
        factor[8 * i : 8 * i + 8, :] = value
    value = factor[...]
    high = value.astype(BF16)
    low = (value - high.astype(F32)).astype(BF16)
    for k in range(2):
        weights[0:128, 128 * k : 128 * k + 128] = high
        weights[128:256, 128 * k : 128 * k + 128] = low
    dims = (((1,), (1,)), ((), ()))
    step = sketch.shape[0] // 4
    for i in range(4):
        at = slice(step * i, step * (i + 1))
        wide = lax.dot_general(sketch[at, :], weights[...], dims, preferred_element_type=F32)
        basis[at, :] = (wide[:, 0:128] + wide[:, 128:256]).astype(BF16)
    projected[...] = lax.dot_general(
        product[...], value, dims, precision=lax.Precision.HIGHEST, preferred_element_type=F32
    ) * (1.0 / total_rows**0.5)


def shape(rows, columns, kind):
    return jax.ShapeDtypeStruct((rows, columns), kind)


def body(slab, test_matrix):
    rows, columns = slab.shape
    width = test_matrix.shape[1]
    total_rows = rows * lax.axis_size("row")
    quarter = rows // Y
    block = quarter + TAIL
    row = lax.axis_index("row")
    me_c = row % C
    me = jnp.stack([lax.axis_index("col"), row // (X * C), (row // C) % X, me_c]).astype(jnp.int32)

    remote, own, held = pl.pallas_call(
        sketch_kernel,
        name="sketch",
        out_shape=(
            jax.ShapeDtypeStruct((3, block, width), F32),
            shape(quarter, width, F32),
            shape(rows, columns, BF16),
        ),
        in_specs=[SMEM, ANY, VMEM],
        out_specs=(VMEM, VMEM, VMEM),
        scratch_shapes=[pltpu.SemaphoreType.DMA((8,))],
        compiler_params=pltpu.CompilerParams(vmem_limit_bytes=40 * MIB),
    )(me, slab, test_matrix)

    received = [
        col_shift(remote[i].astype(F16), dy).astype(F32) for i, dy in enumerate((2, 1, 3))
    ]
    own = pl.pallas_call(
        combine_kernel,
        name="combine",
        out_shape=shape(block, width, F32),
        in_specs=[VMEM] * 4,
        out_specs=VMEM,
    )(own, *received)

    own = own.astype(F16)
    gathered = [own] + [col_shift(own, dy) for dy in (1, 2, 3)]
    pieces, gram, sketch = pl.pallas_call(
        product_kernel,
        name="product",
        out_shape=(
            jax.ShapeDtypeStruct((2, columns // 2, width), F32),
            shape(width, width, F32),
            shape(rows, 2 * width, BF16),
        ),
        in_specs=[SMEM, VMEM] + [VMEM] * 4,
        out_specs=(VMEM, VMEM, VMEM),
        scratch_shapes=[pltpu.VMEM((2 * width, rows), BF16), pltpu.VMEM((width, columns), F32)],
        compiler_params=pltpu.CompilerParams(vmem_limit_bytes=40 * MIB),
    )(me, held, *[piece.astype(F32) for piece in gathered])

    half = width // C

    def half_of(index):
        return lax.dynamic_slice_in_dim(gram, index * half, half, 0)

    def with_gram(a, g):
        return jnp.concatenate([a, g], 0)

    got = row_shift(with_gram(pieces[1], half_of(1 - me_c)), 0, 0, 1)
    mine = pieces[0] + got[:-half]
    part = half_of(me_c) + got[-half:]

    wide = mine.shape[0] // X
    total, gsum = mine[:wide], part
    for dx in (2, 1, 3):
        got = row_shift(with_gram(mine[dx * wide : (dx + 1) * wide], part), 0, dx, 0)
        total, gsum = total + got[:wide], gsum + got[wide:]

    thin = wide // Z
    chunk = [total[thin * i : thin * (i + 1)] for i in range(Z)]
    back = row_shift(jnp.concatenate(chunk[4:7] + [gsum], 0), -3, 0, 0)
    ahead = row_shift(jnp.concatenate(chunk[2:4] + [gsum], 0), 2, 0, 0)
    before = chunk[7] + back[:thin]
    centre = chunk[0] + back[thin : 2 * thin] + ahead[:thin]
    after = chunk[1] + back[2 * thin : 3 * thin] + ahead[thin : 2 * thin]
    gsum = gsum + back[3 * thin :]
    gall = gsum + ahead[2 * thin :]
    left = row_shift(with_gram(before, gsum), -1, 0, 0)
    right = row_shift(with_gram(after, gall), 1, 0, 0)
    product = centre + left[:thin] + right[:thin]
    gsum = gall + left[thin:] + right[thin:]
    other = row_shift(gsum, 0, 0, 1)
    first = me_c == 0
    gram = with_gram(jnp.where(first, gsum, other), jnp.where(first, other, gsum))

    def finish(*refs):
        finish_kernel(total_rows, *refs)

    return pl.pallas_call(
        finish,
        name="finish",
        out_shape=(shape(rows, width, BF16), shape(thin, width, F32)),
        scratch_shapes=[pltpu.VMEM((width, width), F32), pltpu.VMEM((2 * width, 2 * width), BF16)],
        compiler_params=pltpu.CompilerParams(vmem_limit_bytes=40 * MIB),
    )(gram, sketch, product)


def solution(mesh):
    placed = (P("row", "col"), P("col", None))
    return jax.shard_map(
        body,
        mesh=mesh,
        in_specs=placed,
        out_specs=(P("row", None), P(("col", "row"), None)),
        check_vma=False,
    )
```

time: 495 us -> 95.3 us (0.19)
  waiting for transfers between devices: 430 us -> 28.4 us
  starting transfers between devices: 0.3 us -> 29.6 us
  Pallas kernels: 0 us -> 25.3 us
  other arithmetic: 24.6 us -> 4.63 us
  matrix products: 18.8 us -> 0 us
  between operations: 13.8 us -> 0.83 us
    psum x2 -> x0, waiting for transfers between devices: 300 us -> none  [the longest x1 242 us: body(): gram = lax.psum(local_gram, ('row', 'col')) / total_rows]
    unnamed x4 -> x0, waiting for transfers between devices: 130 us -> none
    ppermute x0 -> x15, starting transfers between devices: none -> 29.6 us  [the longest x9 19.5 us: row_shift(): return lax.ppermute(value, 'row', pairs)]
    ppermute x0 -> x15, waiting for transfers between devices: none -> 28.4 us  [the longest x9 15.9 us: row_shift(): return lax.ppermute(value, 'row', pairs)]
    pallas_call x0 -> x4, Pallas kernels: none -> 25.3 us  [the longest x1 9.24 us: body(): pl.pallas_call(sketch_kernel, name='sketch', out_shape=(jax.ShapeDtypeStr...]
    another operation x5 -> x2, other arithmetic: 22.9 us -> 0.15 us  [the longest x1 0.08 us: body(): jnp.stack([lax.axis_index('col'), row // (X * C), row // C % X, me_c])]
    dot_general x4 -> x0, matrix products: 18.5 us -> none  [the longest x1 7.11 us: body(): jnp.dot(slab, test_matrix, preferred_element_type=jnp.float32)]
  transfers between devices with their start and end apart: 3 -> 15, of which waited for: 3 -> 12; matrix products, arithmetic and copies ran while one was open for 0% -> 2% of each run, Pallas kernels for 0% -> 0%
where the time goes in v2:
time: 95.3 us; the launch traced here: 95 us
  starting transfers between devices  29.6 us (31%)
  waiting for transfers between devices  28.4 us (30%)
  Pallas kernels  25.3 us (27%)
  local copies, waits for them, and re-layouts  6.24 us (7%)
  other arithmetic  4.63 us (5%)
    ppermute x9, starting transfers between devices, row_shift(): return lax.ppermute(value, 'row', pairs)  19.5 us
    ppermute x9, waiting for transfers between devices, row_shift(): return lax.ppermute(value, 'row', pairs)  15.9 us
    ppermute x6, waiting for transfers between devices, col_shift(): return lax.ppermute(value, 'col', [(y, (y + dy) % Y) for y in range(Y)])  12.5 us
    ppermute x6, starting transfers between devices, col_shift(): return lax.ppermute(value, 'col', [(y, (y + dy) % Y) for y in range(Y)])  10.1 us
    pallas_call x1, Pallas kernels, body(): pl.pallas_call(sketch_kernel, name='sketch', out_shape=(jax.ShapeDtypeStr...  9.24 us
    pallas_call x1, Pallas kernels, body(): pl.pallas_call(finish, name='finish', out_shape=(shape(rows, width, BF16)...  6.95 us
    pallas_call x1, Pallas kernels, body(): pl.pallas_call(product_kernel, name='product', out_shape=(jax.ShapeDtypeS...  6.9 us
    unnamed x6, local copies, waits for them, and re-layouts  6.04 us
  transfers between devices with their start and end apart: 15, of which 12 were waited for; matrix products, arithmetic and copies ran while one was open for 2% of the time, Pallas kernels for 0%

profile of v2, /device:TPU:1, one launch (start us, length us, event | category | flops | bytes accessed | tf_op | source)
XLA Modules:
  0.0 95.0 jit_solution(12650099056088918536)
XLA Ops:
  1.8 9.2 %sketch.1 = (f32[3,720,128]{2,1,0:T(8,128)S(1)}, f32[704,128]{1,0:T(8,128)S(1)}, bf16[2816,2048]{1,0:T(8,128)(2,1)S(1)}) custom-call(s32[4]{0:T(128)S(1)} %pad_add_fusion.me, bf16[2816,2048]{1,0:T(8,128)(2,1)} %slab.1, bf16[2048,128]{1,0:T(8,128)(2,1)S(1)} %copy-done.1), custom_call_target="tpu_custom_call" | custom-call | tf_op jit(solution)/shard_map/sketch/pallas_call | solution.py:179
  11.1 4.3 %copy-done = bf16[2816,2048]{1,0:T(8,128)(2,1)} copy-done((bf16[2816,2048]{1,0:T(8,128)(2,1)}, bf16[2816,2048]{1,0:T(8,128)(2,1)S(1)}, u32[]{:S(2)}) %copy-start) | copy-done | bytes 11534360
  16.2 3.8 %collective-permute-start = (f16[720,128]{1,0:T(8,128)(2,1)S(1)}, f16[720,128]{1,0:T(8,128)(2,1)S(1)}, u32[]{:S(2)}, u32[]{:S(2)}) collective-permute-start(f16[720,128]{1,0:T(8,128)(2,1)S(1)} %get-tuple-element.20), channel_id=1, source_target_pairs={{0,2},{1,3},{2,0},{3,1},{4,6},{5,7},{6,4},{7,5},{8,10},{9,11},{10,... | collective-permute-start | bytes 552968 | tf_op jit(solution)/shard_map/ppermute | solution.py:32
  20.5 2.3 %collective-permute-start.2 = (f16[720,128]{1,0:T(8,128)(2,1)S(1)}, f16[720,128]{1,0:T(8,128)(2,1)S(1)}, u32[]{:S(2)}, u32[]{:S(2)}) collective-permute-start(f16[720,128]{1,0:T(8,128)(2,1)S(1)} %get-tuple-element.18), channel_id=1, source_target_pairs={{0,3},{1,0},{2,1},{3,2},{4,7},{5,4},{6,5},{7,6},{8,11},{9,8},{10,9... | collective-permute-start | bytes 552968 | tf_op jit(solution)/shard_map/ppermute | solution.py:32
  24.2 4.8 %collective-permute-done.1 = f16[720,128]{1,0:T(8,128)(2,1)S(1)} collective-permute-done((f16[720,128]{1,0:T(8,128)(2,1)S(1)}, f16[720,128]{1,0:T(8,128)(2,1)S(1)}, u32[]{:S(2)}, u32[]{:S(2)}) %collective-permute-start.1) | collective-permute-done | bytes 184352 | tf_op jit(solution)/shard_map/ppermute | solution.py:32
  30.5 2.2 %combine.1 = f32[720,128]{1,0:T(8,128)} custom-call(f32[704,128]{1,0:T(8,128)} %copy-done.2, f32[720,128]{1,0:T(8,128)} %convert_element_type.37.a, f32[720,128]{1,0:T(8,128)} %convert_element_type.39.b, f32[720,128]{1,0:T(8,128)} %convert_element_type.41.c), custom_call_target="tpu_custom_call" | custom-call | tf_op jit(solution)/shard_map/combine/pallas_call | solution.py:196
  34.5 2.0 %collective-permute-start.4 = (f16[720,128]{1,0:T(8,128)(2,1)S(1)}, f16[720,128]{1,0:T(8,128)(2,1)S(1)}, u32[]{:S(2)}, u32[]{:S(2)}) collective-permute-start(f16[720,128]{1,0:T(8,128)(2,1)S(1)} %get-tuple-element.17), channel_id=1, source_target_pairs={{0,2},{1,3},{2,0},{3,1},{4,6},{5,7},{6,4},{7,5},{8,10},{9,11},{10,... | collective-permute-start | bytes 552968 | tf_op jit(solution)/shard_map/ppermute | solution.py:32
  37.4 2.5 %collective-permute-done.3 = f16[720,128]{1,0:T(8,128)(2,1)S(1)} collective-permute-done((f16[720,128]{1,0:T(8,128)(2,1)S(1)}, f16[720,128]{1,0:T(8,128)(2,1)S(1)}, u32[]{:S(2)}, u32[]{:S(2)}) %collective-permute-start.3) | collective-permute-done | bytes 184352 | tf_op jit(solution)/shard_map/ppermute | solution.py:32
  39.9 4.0 %collective-permute-done.4 = f16[720,128]{1,0:T(8,128)(2,1)S(1)} collective-permute-done((f16[720,128]{1,0:T(8,128)(2,1)S(1)}, f16[720,128]{1,0:T(8,128)(2,1)S(1)}, u32[]{:S(2)}, u32[]{:S(2)}) %collective-permute-start.4) | collective-permute-done | bytes 184352 | tf_op jit(solution)/shard_map/ppermute | solution.py:32
  44.5 6.9 %product.1 = (f32[2,1024,128]{2,1,0:T(8,128)S(1)}, f32[128,128]{1,0:T(8,128)S(1)}, bf16[2816,256]{1,0:T(8,128)(2,1)S(1)}) custom-call(s32[4]{0:T(128)S(1)} %pad_add_fusion.me, bf16[2816,2048]{1,0:T(8,128)(2,1)} %copy-done, f32[720,128]{1,0:T(8,128)S(1)} %get-tuple-element.16.p0, f32[720,128]{1,0:T(8,128)S(1)} %convert_element_type.44.p1, ...), custom_call_target="tpu_custom_call" | custom-call | tf_op jit(solution)/shard_map/product/pallas_call | solution.py:206
  52.3 2.2 %collective-permute-start.6 = (f32[1088,128]{1,0:T(8,128)}, f32[1088,128]{1,0:T(8,128)S(1)}, u32[]{:S(2)}, u32[]{:S(2)}) collective-permute-start(f32[1088,128]{1,0:T(8,128)} %pad_maximum_fusion), channel_id=1, source_target_pairs={{0,4},{4,0},{8,12},{12,8},{16,20},{20,16},{24,28},{28,24},{32,36},... | collective-permute-start | bytes 1671176 | tf_op jit(solution)/shard_map/ppermute | solution.py:28
  54.5 1.8 %collective-permute-done.6 = f32[1088,128]{1,0:T(8,128)S(1)} collective-permute-done((f32[1088,128]{1,0:T(8,128)}, f32[1088,128]{1,0:T(8,128)S(1)}, u32[]{:S(2)}, u32[]{:S(2)}) %collective-permute-start.6) | collective-permute-done | bytes 557088 | tf_op jit(solution)/shard_map/ppermute | solution.py:28
  56.4 2.6 %collective-permute-start.7 = (f32[320,128]{1,0:T(8,128)S(1)}, f32[320,128]{1,0:T(8,128)S(1)}, u32[]{:S(2)}, u32[]{:S(2)}) collective-permute-start(f32[320,128]{1,0:T(8,128)S(1)} %get-tuple-element.28), channel_id=1, source_target_pairs={{0,16},{4,20},{8,24},{12,28},{16,0},{20,4},{24,8},{28,12},{32,48},... | collective-permute-start | bytes 491528 | tf_op jit(solution)/shard_map/ppermute | solution.py:28
  59.4 2.4 %collective-permute-start.9 = (f32[320,128]{1,0:T(8,128)S(1)}, f32[320,128]{1,0:T(8,128)S(1)}, u32[]{:S(2)}, u32[]{:S(2)}) collective-permute-start(f32[320,128]{1,0:T(8,128)S(1)} %get-tuple-element.30), channel_id=1, source_target_pairs={{0,24},{4,28},{8,0},{12,4},{16,8},{20,12},{24,16},{28,20},{32,56},... | collective-permute-start | bytes 491528 | tf_op jit(solution)/shard_map/ppermute | solution.py:28
  61.7 1.9 %collective-permute-done.7 = f32[320,128]{1,0:T(8,128)S(1)} collective-permute-done((f32[320,128]{1,0:T(8,128)S(1)}, f32[320,128]{1,0:T(8,128)S(1)}, u32[]{:S(2)}, u32[]{:S(2)}) %collective-permute-start.7) | collective-permute-done | bytes 163872 | tf_op jit(solution)/shard_map/ppermute | solution.py:28
  63.6 4.1 %collective-permute-done.8 = f32[320,128]{1,0:T(8,128)S(1)} collective-permute-done((f32[320,128]{1,0:T(8,128)S(1)}, f32[320,128]{1,0:T(8,128)S(1)}, u32[]{:S(2)}, u32[]{:S(2)}) %collective-permute-start.8) | collective-permute-done | bytes 163872 | tf_op jit(solution)/shard_map/ppermute | solution.py:28
  67.8 5.9 %collective-permute-start.10 = (f32[160,128]{1,0:T(8,128)S(1)}, f32[160,128]{1,0:T(8,128)S(1)}, u32[]{:S(2)}, u32[]{:S(2)}) collective-permute-start(f32[160,128]{1,0:T(8,128)S(1)} %pad_maximum_fusion.4), channel_id=1, source_target_pairs={{0,160},{4,164},{8,168},{12,172},{16,176},{20,180},{24,184},{28,18... | collective-permute-start | bytes 245768 | tf_op jit(solution)/shard_map/ppermute | solution.py:28
  73.8 1.2 %collective-permute-start.11 = (f32[128,128]{1,0:T(8,128)S(1)}, f32[128,128]{1,0:T(8,128)S(1)}, u32[]{:S(2)}, u32[]{:S(2)}) collective-permute-start(f32[128,128]{1,0:T(8,128)S(1)} %pad_maximum_fusion.5), channel_id=1, source_target_pairs={{0,64},{4,68},{8,72},{12,76},{16,80},{20,84},{24,88},{28,92},{32,9... | collective-permute-start | bytes 196616 | tf_op jit(solution)/shard_map/ppermute | solution.py:28
  74.9 4.3 %collective-permute-done.11 = f32[128,128]{1,0:T(8,128)S(1)} collective-permute-done((f32[128,128]{1,0:T(8,128)S(1)}, f32[128,128]{1,0:T(8,128)S(1)}, u32[]{:S(2)}, u32[]{:S(2)}) %collective-permute-start.11) | collective-permute-done | bytes 65568 | tf_op jit(solution)/shard_map/ppermute | solution.py:28
  79.5 1.3 %collective-permute-start.13 = (f32[96,128]{1,0:T(8,128)S(1)}, f32[96,128]{1,0:T(8,128)S(1)}, u32[]{:S(2)}, u32[]{:S(2)}) collective-permute-start(f32[96,128]{1,0:T(8,128)S(1)} %pad_maximum_fusion.8), channel_id=1, source_target_pairs={{0,32},{4,36},{8,40},{12,44},{16,48},{20,52},{24,56},{28,60},{32,6... | collective-permute-start | bytes 147464 | tf_op jit(solution)/shard_map/ppermute | solution.py:28
  80.8 1.5 %collective-permute-done.12 = f32[96,128]{1,0:T(8,128)S(1)} collective-permute-done((f32[96,128]{1,0:T(8,128)S(1)}, f32[96,128]{1,0:T(8,128)S(1)}, u32[]{:S(2)}, u32[]{:S(2)}) %collective-permute-start.12) | collective-permute-done | bytes 49184 | tf_op jit(solution)/shard_map/ppermute | solution.py:28
  82.3 1.5 %collective-permute-done.13 = f32[96,128]{1,0:T(8,128)S(1)} collective-permute-done((f32[96,128]{1,0:T(8,128)S(1)}, f32[96,128]{1,0:T(8,128)S(1)}, u32[]{:S(2)}, u32[]{:S(2)}) %collective-permute-start.13) | collective-permute-done | bytes 49184 | tf_op jit(solution)/shard_map/ppermute | solution.py:28
  83.8 3.4 %collective-permute-start.14 = (f32[64,128]{1,0:T(8,128)S(1)}, f32[64,128]{1,0:T(8,128)S(1)}, u32[]{:S(2)}, u32[]{:S(2)}) collective-permute-start(f32[64,128]{1,0:T(8,128)S(1)} %slice_add_fusion.4), channel_id=1, source_target_pairs={{0,4},{4,0},{8,12},{12,8},{16,20},{20,16},{24,28},{28,24},{32,36},... | collective-permute-start | bytes 98312 | tf_op jit(solution)/shard_map/ppermute | solution.py:28
  88.1 7.0 %finish.1 = (bf16[2816,128]{1,0:T(8,128)(2,1)}, f32[32,128]{1,0:T(8,128)}) custom-call(f32[128,128]{1,0:T(8,128)S(1)} %pad_maximum_fusion.6.refs_0_, bf16[2816,256]{1,0:T(8,128)(2,1)S(1)} %get-tuple-element.13.refs_1_, f32[32,128]{1,0:T(8,128)S(1)} %slice_add_fusion.12.refs_2_), custom_call_target="tpu_custom_call" | custom-call | tf_op jit(solution)/shard_map/finish/pallas_call | solution.py:258
  (47 shorter events, 11.2 us)
Async XLA Ops:
  0.7 1.0 %copy-start.1 = (bf16[2048,128]{1,0:T(8,128)(2,1)S(1)}, bf16[2048,128]{1,0:T(8,128)(2,1)}, u32[]{:S(2)}) copy-start(bf16[2048,128]{1,0:T(8,128)(2,1)} %test.1) | copy-start | bytes 1572868
  11.0 4.3 %copy-start = (bf16[2816,2048]{1,0:T(8,128)(2,1)}, bf16[2816,2048]{1,0:T(8,128)(2,1)S(1)}, u32[]{:S(2)}) copy-start(bf16[2816,2048]{1,0:T(8,128)(2,1)S(1)} %get-tuple-element.8.slab) | copy-start | bytes 34603012
  15.4 0.8 copy-start.2
  16.2 7.2 %collective-permute-start = (f16[720,128]{1,0:T(8,128)(2,1)S(1)}, f16[720,128]{1,0:T(8,128)(2,1)S(1)}, u32[]{:S(2)}, u32[]{:S(2)}) collective-permute-start(f16[720,128]{1,0:T(8,128)(2,1)S(1)} %get-tuple-element.20), channel_id=1, source_target_pairs={{0,2},{1,3},{2,0},{3,1},{4,6},{5,7},{6,4},{7,5},{8,10},{9,11},{10,... | collective-permute-start | bytes 552968 | tf_op jit(solution)/shard_map/ppermute | solution.py:32
  20.1 8.9 %collective-permute-start.1 = (f16[720,128]{1,0:T(8,128)(2,1)S(1)}, f16[720,128]{1,0:T(8,128)(2,1)S(1)}, u32[]{:S(2)}, u32[]{:S(2)}) collective-permute-start(f16[720,128]{1,0:T(8,128)(2,1)S(1)} %get-tuple-element.19), channel_id=1, source_target_pairs={{0,1},{1,2},{2,3},{3,0},{4,5},{5,6},{6,7},{7,4},{8,9},{9,10},{10,1... | collective-permute-start | bytes 552968 | tf_op jit(solution)/shard_map/ppermute | solution.py:32
  20.5 9.3 %collective-permute-start.2 = (f16[720,128]{1,0:T(8,128)(2,1)S(1)}, f16[720,128]{1,0:T(8,128)(2,1)S(1)}, u32[]{:S(2)}, u32[]{:S(2)}) collective-permute-start(f16[720,128]{1,0:T(8,128)(2,1)S(1)} %get-tuple-element.18), channel_id=1, source_target_pairs={{0,3},{1,0},{2,1},{3,2},{4,7},{5,4},{6,5},{7,6},{8,11},{9,8},{10,9... | collective-permute-start | bytes 552968 | tf_op jit(solution)/shard_map/ppermute | solution.py:32
  33.8 6.1 %collective-permute-start.3 = (f16[720,128]{1,0:T(8,128)(2,1)S(1)}, f16[720,128]{1,0:T(8,128)(2,1)S(1)}, u32[]{:S(2)}, u32[]{:S(2)}) collective-permute-start(f16[720,128]{1,0:T(8,128)(2,1)S(1)} %get-tuple-element.17), channel_id=1, source_target_pairs={{0,1},{1,2},{2,3},{3,0},{4,5},{5,6},{6,7},{7,4},{8,9},{9,10},{10,1... | collective-permute-start | bytes 552968 | tf_op jit(solution)/shard_map/ppermute | solution.py:32
  34.5 9.4 %collective-permute-start.4 = (f16[720,128]{1,0:T(8,128)(2,1)S(1)}, f16[720,128]{1,0:T(8,128)(2,1)S(1)}, u32[]{:S(2)}, u32[]{:S(2)}) collective-permute-start(f16[720,128]{1,0:T(8,128)(2,1)S(1)} %get-tuple-element.17), channel_id=1, source_target_pairs={{0,2},{1,3},{2,0},{3,1},{4,6},{5,7},{6,4},{7,5},{8,10},{9,11},{10,... | collective-permute-start | bytes 552968 | tf_op jit(solution)/shard_map/ppermute | solution.py:32
  36.5 8.0 %collective-permute-start.5 = (f16[720,128]{1,0:T(8,128)(2,1)S(1)}, f16[720,128]{1,0:T(8,128)(2,1)S(1)}, u32[]{:S(2)}, u32[]{:S(2)}) collective-permute-start(f16[720,128]{1,0:T(8,128)(2,1)S(1)} %get-tuple-element.17), channel_id=1, source_target_pairs={{0,3},{1,0},{2,1},{3,2},{4,7},{5,4},{6,5},{7,6},{8,11},{9,8},{10,9... | collective-permute-start | bytes 552968 | tf_op jit(solution)/shard_map/ppermute | solution.py:32
  52.3 4.0 %collective-permute-start.6 = (f32[1088,128]{1,0:T(8,128)}, f32[1088,128]{1,0:T(8,128)S(1)}, u32[]{:S(2)}, u32[]{:S(2)}) collective-permute-start(f32[1088,128]{1,0:T(8,128)} %pad_maximum_fusion), channel_id=1, source_target_pairs={{0,4},{4,0},{8,12},{12,8},{16,20},{20,16},{24,28},{28,24},{32,36},... | collective-permute-start | bytes 1671176 | tf_op jit(solution)/shard_map/ppermute | solution.py:28
  56.4 7.2 %collective-permute-start.7 = (f32[320,128]{1,0:T(8,128)S(1)}, f32[320,128]{1,0:T(8,128)S(1)}, u32[]{:S(2)}, u32[]{:S(2)}) collective-permute-start(f32[320,128]{1,0:T(8,128)S(1)} %get-tuple-element.28), channel_id=1, source_target_pairs={{0,16},{4,20},{8,24},{12,28},{16,0},{20,4},{24,8},{28,12},{32,48},... | collective-permute-start | bytes 491528 | tf_op jit(solution)/shard_map/ppermute | solution.py:28
  59.1 8.7 %collective-permute-start.8 = (f32[320,128]{1,0:T(8,128)S(1)}, f32[320,128]{1,0:T(8,128)S(1)}, u32[]{:S(2)}, u32[]{:S(2)}) collective-permute-start(f32[320,128]{1,0:T(8,128)S(1)} %get-tuple-element.29), channel_id=1, source_target_pairs={{0,8},{4,12},{8,16},{12,20},{16,24},{20,28},{24,0},{28,4},{32,40},... | collective-permute-start | bytes 491528 | tf_op jit(solution)/shard_map/ppermute | solution.py:28
  59.4 8.3 %collective-permute-start.9 = (f32[320,128]{1,0:T(8,128)S(1)}, f32[320,128]{1,0:T(8,128)S(1)}, u32[]{:S(2)}, u32[]{:S(2)}) collective-permute-start(f32[320,128]{1,0:T(8,128)S(1)} %get-tuple-element.30), channel_id=1, source_target_pairs={{0,24},{4,28},{8,0},{12,4},{16,8},{20,12},{24,16},{28,20},{32,56},... | collective-permute-start | bytes 491528 | tf_op jit(solution)/shard_map/ppermute | solution.py:28
  67.8 11.4 %collective-permute-start.10 = (f32[160,128]{1,0:T(8,128)S(1)}, f32[160,128]{1,0:T(8,128)S(1)}, u32[]{:S(2)}, u32[]{:S(2)}) collective-permute-start(f32[160,128]{1,0:T(8,128)S(1)} %pad_maximum_fusion.4), channel_id=1, source_target_pairs={{0,160},{4,164},{8,168},{12,172},{16,176},{20,180},{24,184},{28,18... | collective-permute-start | bytes 245768 | tf_op jit(solution)/shard_map/ppermute | solution.py:28
  73.8 5.5 %collective-permute-start.11 = (f32[128,128]{1,0:T(8,128)S(1)}, f32[128,128]{1,0:T(8,128)S(1)}, u32[]{:S(2)}, u32[]{:S(2)}) collective-permute-start(f32[128,128]{1,0:T(8,128)S(1)} %pad_maximum_fusion.5), channel_id=1, source_target_pairs={{0,64},{4,68},{8,72},{12,76},{16,80},{20,84},{24,88},{28,92},{32,9... | collective-permute-start | bytes 196616 | tf_op jit(solution)/shard_map/ppermute | solution.py:28
  79.3 3.0 %collective-permute-start.12 = (f32[96,128]{1,0:T(8,128)S(1)}, f32[96,128]{1,0:T(8,128)S(1)}, u32[]{:S(2)}, u32[]{:S(2)}) collective-permute-start(f32[96,128]{1,0:T(8,128)S(1)} %pad_maximum_fusion.7), channel_id=1, source_target_pairs={{0,224},{4,228},{8,232},{12,236},{16,240},{20,244},{24,248},{28,25... | collective-permute-start | bytes 147464 | tf_op jit(solution)/shard_map/ppermute | solution.py:28
  79.5 4.3 %collective-permute-start.13 = (f32[96,128]{1,0:T(8,128)S(1)}, f32[96,128]{1,0:T(8,128)S(1)}, u32[]{:S(2)}, u32[]{:S(2)}) collective-permute-start(f32[96,128]{1,0:T(8,128)S(1)} %pad_maximum_fusion.8), channel_id=1, source_target_pairs={{0,32},{4,36},{8,40},{12,44},{16,48},{20,52},{24,56},{28,60},{32,6... | collective-permute-start | bytes 147464 | tf_op jit(solution)/shard_map/ppermute | solution.py:28
  83.8 4.2 %collective-permute-start.14 = (f32[64,128]{1,0:T(8,128)S(1)}, f32[64,128]{1,0:T(8,128)S(1)}, u32[]{:S(2)}, u32[]{:S(2)}) collective-permute-start(f32[64,128]{1,0:T(8,128)S(1)} %slice_add_fusion.4), channel_id=1, source_target_pairs={{0,4},{4,0},{8,12},{12,8},{16,20},{20,16},{24,28},{28,24},{32,36},... | collective-permute-start | bytes 98312 | tf_op jit(solution)/shard_map/ppermute | solution.py:28
